TPU v7x, 32 devices: a whole 2x2x4 slice. The times are simulated.
32 devices in a mesh: groups: 2 (over y), band: 4 (over z), dp: 4 (over x, core).
Axes of the slice: x: 2, y: 2, z: 4, core: 2. Of those that a mesh axis runs over, the one named last changes fastest.
Arguments:
- grid_latent: bfloat16 [8, 6144, 512], P(('groups', 'dp'), 'band'), parts along dimension 0, may hold values from -6 to 6
- mesh_latent: bfloat16 [8, 512, 512], P(('groups', 'dp'), 'band'), parts along dimension 0, may hold values from -6 to 6
- cotangent: bfloat16 [8, 512, 512], P(('groups', 'dp'), 'band'), parts along dimension 0, may hold values from -6 to 6
- w_msg: bfloat16 [512, 512], replicated, may hold values from -0.25 to 0.25
- w_self: bfloat16 [512, 512], replicated, may hold values from -0.25 to 0.25
- w_agg: bfloat16 [512, 512], replicated, may hold values from -0.0625 to 0.0625
- w_out: bfloat16 [512, 512], replicated, may hold values from -0.25 to 0.25
- target: int32 [96, 1], P(('groups', 'band')), parts along dimension 0, may hold values from 0 to 3; in each aligned block of 12 rows (0 to 11, 12 to 23, ...) at most 3 rows name the same one
- owner_map: int32 [8], P('groups'), parts along dimension 0, may hold values from 0 to 3, each once
- pattern: int32 [12288, 2], P(('groups', 'band')), parts along dimension 0, may hold values from 0 to 127
- live_blocks: int32 [8], P(('groups', 'band')), parts along dimension 0, may hold values from 6 to 12, as said below
Outputs:
- mesh_out: bfloat16 [8, 512, 512], P(('groups', 'dp'), 'band'), parts along dimension 0
- grad_mesh: bfloat16 [8, 512, 512], P(('groups', 'dp'), 'band'), parts along dimension 0
- grad_grid: bfloat16 [8, 6144, 512], P(('groups', 'dp'), 'band'), parts along dimension 0
- weight_grads: float32 [4096, 512], P(('groups', 'band', 'dp')), parts along dimension 0
There are 2 independent parts, one for each index of `groups`. A program takes and returns all parts, laid end to end along the dimension named above; an argument that names none is the same for every part. Nothing has to cross between parts.
Inputs may be any that keep to these rules, and one draw needn't show every extreme that they name: `target`: in each aligned block of 12 rows (the grid blocks of one band) no mesh block is named more than 3 times, and some mesh block exactly 3 times. `owner_map`: each mesh block has its own position. `live_blocks`: some band has exactly 12 live blocks.
All inputs are finite; a program needn't handle non-finite values.
Results may differ from a plain program's by a relative error of at most 0.0068.
Values may be sent and summed in bfloat16 or wider, within the bound.
A program may use at most 128 MiB of HBM per device.

v0:
```python
import jax
import jax.numpy as jnp
from jax import lax
from jax.sharding import PartitionSpec as P


def silu_slope(value):
    logistic = jax.nn.sigmoid(value)
    return logistic * (1.0 + value * (1.0 - logistic))


def incidence_of(edge_pattern, block_size):
    columns = jnp.arange(block_size, dtype=jnp.int32)
    first_hit = (edge_pattern[..., 0:1] == columns).astype(jnp.bfloat16)
    second_hit = (edge_pattern[..., 1:2] == columns).astype(jnp.bfloat16)
    return first_hit + second_hit


def row_product(left, right):
    return lax.dot_general(
        left, right, (((0,), (0,)), ((), ())), preferred_element_type=jnp.float32
    )


def shards(
    grid_latent,
    mesh_latent,
    cotangent,
    w_msg,
    w_self,
    w_agg,
    w_out,
    target,
    owner_map,
    pattern,
    live_blocks,
):
    grid_rows = grid_latent[0]
    mesh_rows = mesh_latent[0]
    cot_rows = cotangent[0]
    block_count = target.shape[0]
    width = grid_rows.shape[1]
    block_size = grid_rows.shape[0] // block_count
    bands = lax.axis_size("band")
    mesh_blocks = owner_map.shape[0]
    per_band = mesh_blocks // bands
    capacity = (block_count + mesh_blocks - 1) // mesh_blocks
    slot_total = mesh_blocks * capacity
    block_ids = jnp.arange(block_count, dtype=jnp.int32)
    live_flag = block_ids < live_blocks[0]
    matches = target[:, 0][:, None] == jnp.arange(mesh_blocks, dtype=jnp.int32)[None, :]
    mesh_slot = jnp.sum(jnp.where(matches, owner_map[None, :], 0), axis=1)
    same_slot = (
        (mesh_slot[:, None] == mesh_slot[None, :])
        & live_flag[None, :]
        & (block_ids[None, :] < block_ids[:, None])
    )
    slot_rank = jnp.sum(same_slot.astype(jnp.int32), axis=1)
    buffer_index = jnp.where(live_flag, mesh_slot * capacity + slot_rank, slot_total)
    pre_msg = jnp.dot(grid_rows, w_msg, preferred_element_type=jnp.float32)
    messages = jax.nn.silu(pre_msg).astype(jnp.bfloat16).reshape(block_count, block_size, width)
    local_pattern = pattern.reshape(block_count, block_size, 2)
    send_msgs = (
        jnp.zeros((slot_total, block_size, width), jnp.bfloat16)
        .at[buffer_index]
        .set(messages, mode="drop")
    )
    send_pattern = (
        jnp.zeros((slot_total, block_size, 2), jnp.int32)
        .at[buffer_index]
        .set(local_pattern, mode="drop")
    )
    recv_msgs, recv_pattern = (
        lax.all_to_all(send_msgs, "band", split_axis=0, concat_axis=0, tiled=True),
        lax.all_to_all(send_pattern, "band", split_axis=0, concat_axis=0, tiled=True),
    )
    recv_incidence = incidence_of(recv_pattern, block_size).reshape(
        bands, per_band, capacity, block_size, block_size
    )
    aggregate = jnp.einsum(
        "pmcgk,pmcgl->mkl",
        recv_incidence,
        recv_msgs.reshape(bands, per_band, capacity, block_size, width),
        preferred_element_type=jnp.float32,
    )
    agg_half = aggregate.reshape(per_band * block_size, width).astype(jnp.bfloat16)
    pre_hidden = jnp.dot(mesh_rows, w_self, preferred_element_type=jnp.float32) + jnp.dot(
        agg_half, w_agg, preferred_element_type=jnp.float32
    )
    hidden = jax.nn.silu(pre_hidden).astype(jnp.bfloat16)
    mesh_out = (
        mesh_rows.astype(jnp.float32) + jnp.dot(hidden, w_out, preferred_element_type=jnp.float32)
    ).astype(jnp.bfloat16)
    d_hidden = lax.dot_general(
        cot_rows, w_out, (((1,), (1,)), ((), ())), preferred_element_type=jnp.float32
    )
    d_pre_hidden = (d_hidden * silu_slope(pre_hidden)).astype(jnp.bfloat16)
    grad_mesh = (
        cot_rows.astype(jnp.float32)
        + lax.dot_general(
            d_pre_hidden, w_self, (((1,), (1,)), ((), ())), preferred_element_type=jnp.float32
        )
    ).astype(jnp.bfloat16)
    d_aggregate = lax.dot_general(
        d_pre_hidden, w_agg, (((1,), (1,)), ((), ())), preferred_element_type=jnp.float32
    ).astype(jnp.bfloat16)
    d_blocks = d_aggregate.reshape(per_band, block_size, width)
    slot_adjoint = jnp.einsum(
        "pmcgk,mkl->pmcgl", recv_incidence, d_blocks, preferred_element_type=jnp.float32
    )
    returned = lax.all_to_all(
        slot_adjoint.reshape(slot_total, block_size, width),
        "band",
        split_axis=0,
        concat_axis=0,
        tiled=True,
    )
    d_messages = returned[jnp.minimum(buffer_index, slot_total - 1)]
    d_messages = d_messages * live_flag.astype(jnp.float32)[:, None, None]
    d_pre_msg = (d_messages.reshape(block_count * block_size, width) * silu_slope(pre_msg)).astype(
        jnp.bfloat16
    )
    grad_grid = lax.dot_general(
        d_pre_msg, w_msg, (((1,), (1,)), ((), ())), preferred_element_type=jnp.float32
    ).astype(jnp.bfloat16)
    stacked = jnp.concatenate(
        [
            row_product(mesh_rows, d_pre_hidden),
            row_product(agg_half, d_pre_hidden),
            row_product(hidden, cot_rows),
            row_product(grid_rows, d_pre_msg),
        ],
        axis=0,
    )
    weight_grads = lax.psum_scatter(stacked, ("band", "dp"), scatter_dimension=0, tiled=True)
    return (mesh_out[None], grad_mesh[None], grad_grid[None], weight_grads)


def solution(mesh):
    in_specs = (
        P(("groups", "dp"), "band", None),
        P(("groups", "dp"), "band", None),
        P(("groups", "dp"), "band", None),
        P(),
        P(),
        P(),
        P(),
        P(("groups", "band"), None),
        P("groups"),
        P(("groups", "band"), None),
        P(("groups", "band")),
    )
    out_specs = (
        P(("groups", "dp"), "band", None),
        P(("groups", "dp"), "band", None),
        P(("groups", "dp"), "band", None),
        P(("groups", "band", "dp"), None),
    )
    return jax.shard_map(shards, mesh=mesh, in_specs=in_specs, out_specs=out_specs, check_vma=False)
```

profile of v0, /device:TPU:28, one launch (start us, length us, event | category | flops | bytes accessed | tf_op | source)
XLA Modules:
  0.0 244.5 jit_solution(2054253802742438582)
XLA Ops:
  9.5 2.2 scatter_fusion
  11.7 5.1 %all-to-all-start = ((s32[12,128,2]{1,2,0:T(2,128)}), s32[12,128,2]{1,2,0:T(2,128)S(1)}, u32[]{:S(2)}, u32[]{:S(2)}) async-start(s32[12,128,2]{1,2,0:T(2,128)} %scatter_fusion), calls=%async_computation | async-start | bytes 24576 | tf_op jit(solution)/shard_map/all_to_all | solution.py:75
  16.8 4.5 %multiply_convert_fusion = (bf16[1536,512]{1,0:T(8,128)(2,1)}, f32[1536,512]{1,0:T(8,128)}) fusion(bf16[512,512]{1,0:T(8,128)(2,1)} %param.14, bf16[1,1536,512]{2,1,0:T(8,128)(2,1)S(1)} %copy-done), kind=kOutput, calls=%fused_computation.7 | convolution fusion | flops 809238528 | bytes 6815744 | tf_op jit(solution)/shard_map/dot_general | solution.py:60
  21.3 1.3 broadcast_in_dim.48
  22.6 5.0 %scatter_fusion.1 = bf16[12,128,512]{2,1,0:T(8,128)(2,1)} fusion(bf16[12,128,512]{2,1,0:T(8,128)(2,1)} %broadcast_in_dim.48, s32[12]{0:T(128)S(1)} %fusion.37, bf16[12,128,512]{2,1,0:T(8,128)(2,1)} %bitcast.87), kind=kCustom, calls=%fused_computation.2 | custom fusion | bytes 4718640 | tf_op jit(solution)/shard_map/scatter | solution.py:66
  27.6 5.2 %all-to-all-start.1 = ((bf16[12,128,512]{2,1,0:T(8,128)(2,1)}), bf16[12,128,512]{2,1,0:T(8,128)(2,1)}, u32[]{:S(2)}, u32[]{:S(2)}) async-start(bf16[12,128,512]{2,1,0:T(8,128)(2,1)} %scatter_fusion.1), calls=%async_computation.1 | async-start | bytes 3145728 | tf_op jit(solution)/shard_map/all_to_all | solution.py:74
  33.2 34.1 %all-to-all-done.1 = bf16[12,128,512]{2,1,0:T(8,128)(2,1)} async-done(((bf16[12,128,512]{2,1,0:T(8,128)(2,1)}), bf16[12,128,512]{2,1,0:T(8,128)(2,1)}, u32[]{:S(2)}, u32[]{:S(2)}) %all-to-all-start.1) | async-done | bytes 1572896 | tf_op jit(solution)/shard_map/all_to_all | solution.py:74
  67.3 2.5 %fusion.18 = bf16[128,512]{1,0:T(8,128)(2,1)S(1)} fusion(bf16[4,3,128,512]{3,2,1,0:T(8,128)(2,1)} %bitcast.8, s32[4,3,128]{2,1,0:T(4,128)S(1)} %eq.75, s32[4,3,128]{2,1,0:T(4,128)S(1)} %eq.71), kind=kOutput, calls=%fused_computation.28 | convolution fusion | flops 202964992 | bytes 1716224 | tf_op jit(solution)/shard_map/pmcgk,pmcgl->mkl/dot_general | solution.py:80
  71.1 2.8 %fusion.26 = f32[512,4,3,128]{3,0,2,1:T(8,128)} fusion(bf16[128,512]{1,0:T(8,128)(2,1)S(1)} %fusion.16, bf16[512,512]{1,0:T(8,128)(2,1)S(1)} %copy-done.4, s32[4,3,128]{2,1,0:T(4,128)S(1)} %eq.75, s32[4,3,128]{2,1,0:T(4,128)S(1)} %eq.71), kind=kOutput, calls=%fused_computation.36 | convolution fusion | flops 270073856 | bytes 3813376 | tf_op jit(solution)/shard_map/pmcgk,mkl->pmcgl/dot_general | solution.py:108
  73.9 3.6 %copy.25 = f32[12,128,512]{2,1,0:T(8,128)} copy(f32[12,128,512]{1,2,0:T(8,128)} %bitcast.86) | data formatting | bytes 6291456 | tf_op jit(solution)/shard_map/reshape | solution.py:112
  77.5 7.0 %all-to-all-start.2 = ((f32[12,128,512]{2,1,0:T(8,128)}), f32[12,128,512]{2,1,0:T(8,128)}, u32[]{:S(2)}, u32[]{:S(2)}) async-start(f32[12,128,512]{2,1,0:T(8,128)} %copy.25), calls=%async_computation.2 | async-start | bytes 6291456 | tf_op jit(solution)/shard_map/all_to_all | solution.py:111
  84.5 1.2 fusion.40
  85.8 2.2 convolution_bitcast_fusion
  88.0 2.2 fusion.29
  90.2 62.2 %all-to-all-done.2 = f32[12,128,512]{2,1,0:T(8,128)} async-done(((f32[12,128,512]{2,1,0:T(8,128)}), f32[12,128,512]{2,1,0:T(8,128)}, u32[]{:S(2)}, u32[]{:S(2)}) %all-to-all-start.2) | async-done | bytes 3145760 | tf_op jit(solution)/shard_map/all_to_all | solution.py:111
  152.4 4.3 %gather_fusion = f32[12,128,512]{2,1,0:T(8,128)} fusion(f32[12,128,512]{2,1,0:T(8,128)} %all-to-all-done.2, s32[1024]{0:T(1024)S(1)} %pad_clamp_fusion), kind=kCustom, calls=%fused_computation | custom fusion | bytes 6291504 | tf_op jit(solution)/shard_map/gather | solution.py:118
  156.7 3.6 %fusion.1 = bf16[1536,512]{1,0:T(8,128)(2,1)S(1)} fusion(f32[12,128,512]{2,1,0:T(8,128)} %gather_fusion, f32[1536,512]{1,0:T(8,128)} %get-tuple-element.9, f32[1536]{0:T(1024)S(1)} %broadcast_bitcast_fusion), kind=kLoop, calls=%fused_computation.6 | loop fusion | flops 7864320 | bytes 7870464 | tf_op jit(solution)/shard_map/convert_element_type | solution.py:120
  160.3 1.2 copy-done.5
  161.5 1.0 fusion.9
  163.0 2.4 pad_maximum_fusion
  166.3 1.0 fusion.22
  167.3 0.9 fusion.23
  168.2 3.7 %fusion.2 = bf16[1,1536,512]{2,1,0:T(8,128)(2,1)} fusion(bf16[1536,512]{1,0:T(8,128)(2,1)} %copy-done.5, bf16[512,512]{1,0:T(8,128)(2,1)} %param.14), kind=kOutput, calls=%fused_computation.10 | convolution fusion | flops 806092800 | bytes 3670016 | tf_op jit(solution)/shard_map/dot_general | solution.py:123
  171.9 65.8 %reduce-scatter.2.cloned.1.call-done = f32[128,512]{1,0:T(8,128)} async-done(((f32[2048,512]{1,0:T(8,128)}), f32[128,512]{1,0:T(8,128)}) %reduce-scatter.2.cloned.1.call-update) | async-done | bytes 262160 | tf_op jit(solution)/shard_map/reduce_scatter | solution.py:135
  (43 shorter events, 4.6 us)
Async XLA Ops:
  7.2 9.6 %copy-start = (bf16[1,1536,512]{2,1,0:T(8,128)(2,1)S(1)}, bf16[1,1536,512]{2,1,0:T(8,128)(2,1)}, u32[]{:S(2)}) copy-start(bf16[1,1536,512]{2,1,0:T(8,128)(2,1)} %param.11) | copy-start | bytes 4718596
  11.7 15.9 %all-to-all-start = ((s32[12,128,2]{1,2,0:T(2,128)}), s32[12,128,2]{1,2,0:T(2,128)S(1)}, u32[]{:S(2)}, u32[]{:S(2)}) async-start(s32[12,128,2]{1,2,0:T(2,128)} %scatter_fusion), calls=%async_computation | async-start | bytes 24576 | tf_op jit(solution)/shard_map/all_to_all | solution.py:75
  22.6 10.3 %copy-start.3 = (bf16[512,512]{1,0:T(8,128)(2,1)S(1)}, bf16[512,512]{1,0:T(8,128)(2,1)}, u32[]{:S(2)}) copy-start(bf16[512,512]{1,0:T(8,128)(2,1)} %param.15) | copy-start | bytes 1572868
  22.6 10.3 %copy-start.6 = (bf16[1,128,512]{2,1,0:T(8,128)(2,1)S(1)}, bf16[1,128,512]{2,1,0:T(8,128)(2,1)}, u32[]{:S(2)}) copy-start(bf16[1,128,512]{2,1,0:T(8,128)(2,1)} %param.12) | copy-start | bytes 393220
  27.6 42.9 %copy-start.4 = (bf16[512,512]{1,0:T(8,128)(2,1)S(1)}, bf16[512,512]{1,0:T(8,128)(2,1)}, u32[]{:S(2)}) copy-start(bf16[512,512]{1,0:T(8,128)(2,1)} %param.16) | copy-start | bytes 1572868
  27.6 39.6 %all-to-all-start.1 = ((bf16[12,128,512]{2,1,0:T(8,128)(2,1)}), bf16[12,128,512]{2,1,0:T(8,128)(2,1)}, u32[]{:S(2)}, u32[]{:S(2)}) async-start(bf16[12,128,512]{2,1,0:T(8,128)(2,1)} %scatter_fusion.1), calls=%async_computation.1 | async-start | bytes 3145728 | tf_op jit(solution)/shard_map/all_to_all | solution.py:74
  32.9 37.8 %copy-start.9 = (bf16[1,128,512]{2,1,0:T(8,128)(2,1)S(1)}, bf16[1,128,512]{2,1,0:T(8,128)(2,1)}, u32[]{:S(2)}) copy-start(bf16[1,128,512]{2,1,0:T(8,128)(2,1)} %param.13) | copy-start | bytes 393220
  67.3 3.5 %copy-start.11 = (bf16[512,512]{1,0:T(8,128)(2,1)S(1)}, bf16[512,512]{1,0:T(8,128)(2,1)}, u32[]{:S(2)}) copy-start(bf16[512,512]{1,0:T(8,128)(2,1)} %param.17) | copy-start | bytes 1572868
  69.8 0.7 copy-start.8
  77.5 74.9 %all-to-all-start.2 = ((f32[12,128,512]{2,1,0:T(8,128)}), f32[12,128,512]{2,1,0:T(8,128)}, u32[]{:S(2)}, u32[]{:S(2)}) async-start(f32[12,128,512]{2,1,0:T(8,128)} %copy.25), calls=%async_computation.2 | async-start | bytes 6291456 | tf_op jit(solution)/shard_map/all_to_all | solution.py:111
  84.5 153.2 %reduce-scatter.2.cloned.1.call-start = ((), (), s32[]{:S(2)}) async-start(), calls=%async_computation.4 | async-start | bytes 4456448 | tf_op jit(solution)/shard_map/reduce_scatter | solution.py:135
  160.3 1.2 copy-start.5
  161.5 1.2 copy-start.1
  161.5 1.5 copy-start.2
  165.4 0.9 copy-start.10
  165.4 1.9 copy-start.7
  165.4 1.9 copy-start.12
Sparse Core Ops, SparseCore 0:
  165.6 72.0 reduce-scatter.1
where the time goes:
time: 248 us; the launch traced here: 244 us
  waiting for transfers between devices  162 us (65%)
  matrix products  22.8 us (9%)
  local copies, waits for them, and re-layouts  20.4 us (8%)
  starting transfers between devices  17.3 us (7%)
  between operations  14.9 us (6%)
  other arithmetic  6.92 us (3%)
    reduce_scatter x1, waiting for transfers between devices, shards(): lax.psum_scatter(stacked, ('band', 'dp'), scatter_dimension=0, tiled=True)  65.8 us
    all_to_all x1, waiting for transfers between devices, shards(): lax.all_to_all(slot_adjoint.reshape(slot_total, block_size, width), 'band...  62.2 us
    all_to_all x1, waiting for transfers between devices, shards(): lax.all_to_all(send_msgs, 'band', split_axis=0, concat_axis=0, tiled=True)  34.1 us
    all_to_all x1, starting transfers between devices, shards(): lax.all_to_all(slot_adjoint.reshape(slot_total, block_size, width), 'band...  6.99 us
    dot_general x4, matrix products, row_product(): lax.dot_general(left, right, (((0,), (0,)), ((), ())), preferred_element_...  6.66 us
    all_to_all x1, starting transfers between devices, shards(): lax.all_to_all(send_msgs, 'band', split_axis=0, concat_axis=0, tiled=True)  5.23 us
    all_to_all x1, starting transfers between devices, shards(): lax.all_to_all(send_pattern, 'band', split_axis=0, concat_axis=0, tiled=T...  5.09 us
    scatter x1, local copies, waits for them, and re-layouts, shards(): send_msgs = jnp.zeros((slot_total, block_size, width), jnp.bfloat16).at[b...  5.04 us
  transfers between devices with their start and end apart: 4, of which 3 were waited for; matrix products, arithmetic and copies ran while one was open for 9% of the time, Pallas kernels for 0%

commit v1 on v0

--- a/solution.py
+++ b/solution.py
@@ -1,7 +1,14 @@
+import functools
 import jax
 import jax.numpy as jnp
 from jax import lax
+from jax.experimental import pallas as pl
+from jax.experimental.pallas import tpu as pltpu
 from jax.sharding import PartitionSpec as P
+
+MESH = pl.DeviceIdType.MESH
+F32 = jnp.float32
+BF16 = jnp.bfloat16
 
 
 def silu_slope(value):
@@ -136,6 +143,450 @@
     return (mesh_out[None], grad_mesh[None], grad_grid[None], weight_grads)
 
 
+def mm(left, right):
+    return jnp.dot(left, right, preferred_element_type=F32)
+
+
+def mm_t(left, right):
+    return lax.dot_general(left, right, (((1,), (1,)), ((), ())), preferred_element_type=F32)
+
+
+def logistic_of(value):
+    return 0.5 + 0.5 * jnp.tanh(0.5 * value)
+
+
+def fused(
+    bands,
+    tile,
+    target_s,
+    owner_s,
+    live_s,
+    pattern_t,
+    pattern,
+    grid_h,
+    mesh_h,
+    cot_h,
+    wm_h,
+    ws_h,
+    wa_h,
+    wo_h,
+    mesh_out_h,
+    grad_mesh_h,
+    grad_grid_h,
+    wg_h,
+    grid_v,
+    mesh_v,
+    cot_v,
+    wm_v,
+    ws_v,
+    wa_v,
+    wo_v,
+    hits,
+    hits_t,
+    grid_t,
+    msgs,
+    slope,
+    part,
+    part_send,
+    part_recv,
+    dagg_all,
+    dpm,
+    gg_v,
+    mesh_out_v,
+    grad_mesh_v,
+    sums,
+    send_a,
+    recv_a,
+    send_b,
+    recv_b,
+    send_c,
+    recv_c,
+    total_c,
+    wg_v,
+    in_sem,
+    grid_sem,
+    out_sem,
+    gg_sem,
+    part_ss,
+    part_rs,
+    dagg_ss,
+    dagg_rs,
+    a_ss,
+    a_rs,
+    b_ss,
+    b_rs,
+    c_ss,
+    c_rs,
+):
+    me = lax.axis_index("band")
+    dp = lax.axis_index("dp")
+    core = dp % 2
+    column = dp // 2
+    core_mate = dp + 1 - 2 * core
+    x_mate = (dp + 2) % 4
+    nodes, width = grid_v.shape
+    block = mesh_v.shape[0]
+    mesh_rows = hits.shape[0]
+    tiles = nodes // tile
+    half = width // 2
+    blocks = nodes // block
+
+    loads = [
+        pltpu.make_async_copy(src, dst, in_sem.at[i])
+        for i, (src, dst) in enumerate(
+            ((wm_h, wm_v), (mesh_h, mesh_v), (cot_h, cot_v), (ws_h, ws_v), (wa_h, wa_v), (wo_h, wo_v))
+        )
+    ]
+
+    def grid_load(t):
+        rows = pl.ds(t * tile, tile)
+        return pltpu.make_async_copy(grid_h.at[rows], grid_v.at[rows], grid_sem.at[t])
+
+    loads[0].start()
+    for t in range(tiles):
+        grid_load(t).start()
+    for load in loads[1:]:
+        load.start()
+
+    barrier = pltpu.get_barrier_semaphore()
+    for rel in range(1, bands):
+        pl.semaphore_signal(
+            barrier, inc=1, device_id={"band": (me + rel) % bands}, device_id_type=MESH
+        )
+    pl.semaphore_signal(barrier, inc=1, device_id={"dp": core_mate}, device_id_type=MESH)
+    pl.semaphore_signal(barrier, inc=1, device_id={"dp": x_mate}, device_id_type=MESH)
+
+    live = live_s[0]
+    offsets = []
+    for k in range(blocks):
+        position = owner_s[target_s[k]]
+        offsets.append(jnp.where(k < live, position * block, -2 * mesh_rows))
+    row_ids = lax.broadcasted_iota(jnp.int32, (mesh_rows, block), 0)
+    for k in range(blocks):
+        cols = pl.ds(k * block, block)
+        first = pattern_t[0:1, cols] + offsets[k]
+        second = pattern_t[1:2, cols] + offsets[k]
+        hits[:, cols] = (
+            (row_ids == first).astype(F32) + (row_ids == second).astype(F32)
+        ).astype(BF16)
+
+    loads[0].wait()
+
+    @pl.loop(0, tiles)
+    def _(t):
+        rows = pl.ds(pl.multiple_of(t * tile, tile), tile)
+        grid_load(t).wait()
+        pre = mm(grid_v[rows, :], wm_v[...])
+        gate = logistic_of(pre)
+        msgs[rows, :] = (pre * gate).astype(BF16)
+        slope[rows, :] = gate * (1.0 + pre * (1.0 - gate))
+
+    def part_copy(h, rel):
+        other = (me + rel) % bands
+        return pltpu.make_async_remote_copy(
+            src_ref=part_send.at[h, pl.ds(pl.multiple_of(other * block, block), block)],
+            dst_ref=part_recv.at[h, rel - 1],
+            send_sem=part_ss.at[h, rel - 1],
+            recv_sem=part_rs.at[h, rel - 1],
+            device_id={"band": other},
+            device_id_type=MESH,
+        )
+
+    rels = (2, 1, 3)
+    for h in range(2):
+        cols = slice(h * half, (h + 1) * half)
+        partial = mm(hits[...], msgs[:, cols])
+        part[:, cols] = partial
+        part_send[h] = partial.astype(BF16)
+        if h == 0:
+            pl.semaphore_wait(barrier, bands + 1)
+        for rel in rels:
+            part_copy(h, rel).start()
+
+    for load in loads[1:]:
+        load.wait()
+    mesh_rows_v = mesh_v[...]
+    cot_rows = cot_v[...]
+    pre_self = mm(mesh_rows_v, ws_v[...])
+    d_hidden = mm_t(cot_rows, wo_v[...])
+
+    col_ids = lax.broadcasted_iota(jnp.int32, (block, mesh_rows), 1)
+    for k in range(blocks):
+        rows = pl.ds(k * block, block)
+        first = pattern[rows, 0:1] + offsets[k]
+        second = pattern[rows, 1:2] + offsets[k]
+        hits_t[rows, :] = (
+            (col_ids == first).astype(F32) + (col_ids == second).astype(F32)
+        ).astype(BF16)
+    for t in range(tiles):
+        grid_t[:, t * tile : (t + 1) * tile] = grid_v[t * tile : (t + 1) * tile, :].T
+
+    own = pl.ds(pl.multiple_of(me * block, block), block)
+    agg_parts = []
+    for h in range(2):
+        total = part[own, h * half : (h + 1) * half]
+        for rel in rels:
+            part_copy(h, rel).wait_recv()
+            total = total + part_recv[h, rel - 1].astype(F32)
+        agg_parts.append(total.astype(BF16))
+    agg = jnp.concatenate(agg_parts, axis=1)
+    pre_hidden = pre_self + mm(agg, wa_v[...])
+    gate = logistic_of(pre_hidden)
+    hidden = (pre_hidden * gate).astype(BF16)
+    dph = (d_hidden * (gate * (1.0 + pre_hidden * (1.0 - gate)))).astype(BF16)
+    dagg_all[own, :] = mm_t(dph, wa_v[...]).astype(BF16)
+
+    def dagg_copy(rel):
+        return pltpu.make_async_remote_copy(
+            src_ref=dagg_all.at[own],
+            dst_ref=dagg_all.at[own],
+            send_sem=dagg_ss.at[rel - 1],
+            recv_sem=dagg_rs.at[rel - 1],
+            device_id={"band": (me + rel) % bands},
+            device_id_type=MESH,
+        )
+
+    for rel in rels:
+        dagg_copy(rel).start()
+
+    def a_copy(b):
+        return pltpu.make_async_remote_copy(
+            src_ref=send_a.at[b],
+            dst_ref=recv_a.at[b],
+            send_sem=a_ss.at[b],
+            recv_sem=a_rs.at[b],
+            device_id={"dp": core_mate},
+            device_id_type=MESH,
+        )
+
+    def b_copy(b):
+        return pltpu.make_async_remote_copy(
+            src_ref=send_b.at[b],
+            dst_ref=recv_b.at[b],
+            send_sem=b_ss.at[b],
+            recv_sem=b_rs.at[b],
+            device_id={"dp": x_mate},
+            device_id_type=MESH,
+        )
+
+    def c_copy(rel):
+        other = (me + rel) % bands
+        return pltpu.make_async_remote_copy(
+            src_ref=send_c.at[other],
+            dst_ref=recv_c.at[rel - 1],
+            send_sem=c_ss.at[rel - 1],
+            recv_sem=c_rs.at[rel - 1],
+            device_id={"band": other},
+            device_id_type=MESH,
+        )
+
+    share = width // 4
+
+    def share_of(b, x, c):
+        return sums[b, pl.ds(pl.multiple_of((x * 2 + c) * share, share), share), :]
+
+    def step_a(b):
+        for x in range(2):
+            send_a[b, x] = share_of(b, x, 1 - core).astype(BF16)
+        a_copy(b).start()
+
+    def step_b(b):
+        a_copy(b).wait_recv()
+        away = 1 - column
+        send_b[b] = (share_of(b, away, core) + recv_a[b, away].astype(F32)).astype(BF16)
+        b_copy(b).start()
+
+    def step_c(b):
+        kept = share_of(b, column, core) + recv_a[b, column].astype(F32)
+        b_copy(b).wait_recv()
+        kept = kept + recv_b[b].astype(F32)
+        total_c[b] = kept
+        send_c[b] = kept.astype(BF16)
+
+    sums[0] = row_product(mesh_rows_v, dph)
+    step_a(0)
+    sums[1] = row_product(agg, dph)
+    step_a(1)
+    sums[2] = row_product(hidden, cot_rows)
+    step_a(2)
+    mesh_out_v[...] = (mesh_rows_v.astype(F32) + mm(hidden, wo_v[...])).astype(BF16)
+    grad_mesh_v[...] = (cot_rows.astype(F32) + mm_t(dph, ws_v[...])).astype(BF16)
+    stores = [
+        pltpu.make_async_copy(mesh_out_v, mesh_out_h, out_sem.at[0]),
+        pltpu.make_async_copy(grad_mesh_v, grad_mesh_h, out_sem.at[1]),
+    ]
+    for store in stores:
+        store.start()
+    for b in range(3):
+        step_b(b)
+    for b in range(3):
+        step_c(b)
+    for rel in rels:
+        dagg_copy(rel).wait_recv()
+    for rel in rels:
+
+        @pl.when((me + rel) % bands != 3)
+        def _():
+            c_copy(rel).start()
+
+    @pl.loop(0, tiles)
+    def _(t):
+        rows = pl.ds(pl.multiple_of(t * tile, tile), tile)
+        d_msg = mm(hits_t[rows, :], dagg_all[...])
+        dpm[rows, :] = (d_msg * slope[rows, :]).astype(BF16)
+
+    for h in range(2):
+        cols = slice(h * half, (h + 1) * half)
+        sums[3, :, cols] = mm(grid_t[...], dpm[:, cols])
+    step_a(3)
+
+    def gg_store(t):
+        rows = pl.ds(pl.multiple_of(t * tile, tile), tile)
+        return pltpu.make_async_copy(gg_v.at[rows], grad_grid_h.at[rows], gg_sem.at[t])
+
+    def grid_grads(low, high):
+        @pl.loop(low, high)
+        def _(t):
+            rows = pl.ds(pl.multiple_of(t * tile, tile), tile)
+            gg_v[rows, :] = mm_t(dpm[rows, :], wm_v[...]).astype(BF16)
+            gg_store(t).start()
+
+    grid_grads(0, tiles // 3)
+    step_b(3)
+    grid_grads(tiles // 3, tiles)
+    step_c(3)
+    for rel in rels:
+
+        @pl.when((me + rel) % bands == 3)
+        def _():
+            c_copy(rel).start()
+
+    total = total_c[me]
+    for rel in rels:
+        c_copy(rel).wait_recv()
+        total = total + recv_c[rel - 1].astype(F32)
+    wg_v[...] = total
+    last = pltpu.make_async_copy(wg_v, wg_h, out_sem.at[2])
+    last.start()
+    for store in stores:
+        store.wait()
+
+    @pl.loop(0, tiles)
+    def _(t):
+        gg_store(t).wait()
+
+    for rel in rels:
+        for h in range(2):
+            part_copy(h, rel).wait_send()
+        dagg_copy(rel).wait_send()
+        c_copy(rel).wait_send()
+    for b in range(4):
+        a_copy(b).wait_send()
+        b_copy(b).wait_send()
+    last.wait()
+
+
+def fused_shards(
+    grid_latent,
+    mesh_latent,
+    cotangent,
+    w_msg,
+    w_self,
+    w_agg,
+    w_out,
+    target,
+    owner_map,
+    pattern,
+    live_blocks,
+):
+    bands = lax.axis_size("band")
+    nodes, width = grid_latent.shape[1:]
+    block = mesh_latent.shape[1]
+    rows = bands * block
+    tile = 2 * block
+    tiles = nodes // tile
+    half = width // 2
+    share = width // 4
+    anywhere = pl.BlockSpec(memory_space=pl.ANY)
+    scalars = pl.BlockSpec(memory_space=pltpu.SMEM)
+    local = pl.BlockSpec(memory_space=pltpu.VMEM)
+    dma = pltpu.SemaphoreType.DMA
+    mesh_out, grad_mesh, grad_grid, weight_grads = pl.pallas_call(
+        functools.partial(fused, bands, tile),
+        out_shape=(
+            jax.ShapeDtypeStruct((block, width), BF16),
+            jax.ShapeDtypeStruct((block, width), BF16),
+            jax.ShapeDtypeStruct((nodes, width), BF16),
+            jax.ShapeDtypeStruct((share, width), F32),
+        ),
+        in_specs=[scalars] * 3 + [local] * 2 + [anywhere] * 7,
+        out_specs=(anywhere,) * 4,
+        scratch_shapes=[
+            pltpu.VMEM((nodes, width), BF16),
+            pltpu.VMEM((block, width), BF16),
+            pltpu.VMEM((block, width), BF16),
+            pltpu.VMEM((width, width), BF16),
+            pltpu.VMEM((width, width), BF16),
+            pltpu.VMEM((width, width), BF16),
+            pltpu.VMEM((width, width), BF16),
+            pltpu.VMEM((rows, nodes), BF16),
+            pltpu.VMEM((nodes, rows), BF16),
+            pltpu.VMEM((width, nodes), BF16),
+            pltpu.VMEM((nodes, width), BF16),
+            pltpu.VMEM((nodes, width), F32),
+            pltpu.VMEM((rows, width), F32),
+            pltpu.VMEM((2, rows, half), BF16),
+            pltpu.VMEM((2, bands - 1, block, half), BF16),
+            pltpu.VMEM((rows, width), BF16),
+            pltpu.VMEM((nodes, width), BF16),
+            pltpu.VMEM((nodes, width), BF16),
+            pltpu.VMEM((block, width), BF16),
+            pltpu.VMEM((block, width), BF16),
+            pltpu.VMEM((4, width, width), F32),
+            pltpu.VMEM((4, 2, share, width), BF16),
+            pltpu.VMEM((4, 2, share, width), BF16),
+            pltpu.VMEM((4, share, width), BF16),
+            pltpu.VMEM((4, share, width), BF16),
+            pltpu.VMEM((4, share, width), BF16),
+            pltpu.VMEM((bands - 1, share, width), BF16),
+            pltpu.VMEM((4, share, width), F32),
+            pltpu.VMEM((share, width), F32),
+            dma((6,)),
+            dma((tiles,)),
+            dma((3,)),
+            dma((tiles,)),
+            dma((2, bands - 1)),
+            dma((2, bands - 1)),
+            dma((bands - 1,)),
+            dma((bands - 1,)),
+            dma((4,)),
+            dma((4,)),
+            dma((4,)),
+            dma((4,)),
+            dma((bands - 1,)),
+            dma((bands - 1,)),
+        ],
+        compiler_params=pltpu.CompilerParams(
+            collective_id=0, has_side_effects=True, vmem_limit_bytes=50 * 2**20
+        ),
+        name="encoder_step",
+    )(
+        target[:, 0],
+        owner_map,
+        live_blocks,
+        pattern.T,
+        pattern,
+        grid_latent[0],
+        mesh_latent[0],
+        cotangent[0],
+        w_msg,
+        w_self,
+        w_agg,
+        w_out,
+    )
+    return mesh_out[None], grad_mesh[None], grad_grid[None], weight_grads
+
+
 def solution(mesh):
     in_specs = (
         P(("groups", "dp"), "band", None),
@@ -156,4 +607,5 @@
         P(("groups", "dp"), "band", None),
         P(("groups", "band", "dp"), None),
     )
-    return jax.shard_map(shards, mesh=mesh, in_specs=in_specs, out_specs=out_specs, check_vma=False)
+    body = fused_shards if mesh.shape["band"] == 4 and mesh.shape["dp"] == 4 else shards
+    return jax.shard_map(body, mesh=mesh, in_specs=in_specs, out_specs=out_specs, check_vma=False)

time: 248 us -> 65.9 us (0.27); the launches traced: 244 us -> 65.4 us
  waiting for transfers between devices: 162 us -> 0 us
  Pallas kernels: 0 us -> 50.4 us
  matrix products: 22.8 us -> 0 us
  starting transfers between devices: 17.3 us -> 0 us
  between operations: 14.9 us -> 1.31 us
  other arithmetic: 6.92 us -> 0 us
  local copies, waits for them, and re-layouts: 20.4 us -> 13.6 us
    all_to_all x3 -> x0, waiting for transfers between devices: 96.3 us -> none  [the longest x1 62.2 us: shards(): lax.all_to_all(slot_adjoint.reshape(slot_total, block_size, width), 'band...]
    reduce_scatter x1 -> x0, waiting for transfers between devices: 65.8 us -> none  [shards(): lax.psum_scatter(stacked, ('band', 'dp'), scatter_dimension=0, tiled=True)]
    pallas_call x0 -> x1, Pallas kernels: none -> 50.4 us  [fused_shards(): pl.pallas_call(functools.partial(fused, bands, tile), out_shape=(jax.Shap...]
    dot_general x13 -> x0, matrix products: 22.8 us -> none  [the longest x4 6.66 us: row_product(): lax.dot_general(left, right, (((0,), (0,)), ((), ())), preferred_element_...]
    all_to_all x3 -> x0, starting transfers between devices: 17.3 us -> none  [the longest x1 6.99 us: shards(): lax.all_to_all(slot_adjoint.reshape(slot_total, block_size, width), 'band...]
    unnamed x26 -> x23, local copies, waits for them, and re-layouts: 3.24 us -> 13.6 us
    scatter x2 -> x0, local copies, waits for them, and re-layouts: 7.21 us -> none  [the longest x1 5.04 us: shards(): send_msgs = jnp.zeros((slot_total, block_size, width), jnp.bfloat16).at[b...]
    gather x1 -> x0, local copies, waits for them, and re-layouts: 4.34 us -> none  [shards(): d_messages = returned[jnp.minimum(buffer_index, slot_total - 1)]]
  transfers between devices with their start and end apart: 4 -> 0, of which waited for: 3 -> 0; matrix products, arithmetic and copies ran while one was open for 9% -> 0% of each run, Pallas kernels for 0% -> 0%
where the time goes in v1:
time: 65.9 us; the launch traced here: 65.4 us
  Pallas kernels  50.4 us (76%)
  local copies, waits for them, and re-layouts  13.6 us (21%)
  between operations  1.31 us (2%)
    pallas_call x1, Pallas kernels, fused_shards(): pl.pallas_call(functools.partial(fused, bands, tile), out_shape=(jax.Shap...  50.4 us
    unnamed x23, local copies, waits for them, and re-layouts  13.6 us

profile of v1, /device:TPU:28, one launch (start us, length us, event | category | flops | bytes accessed | tf_op | source)
XLA Modules:
  0.0 65.4 jit_solution(8870337906118438011)
XLA Ops:
  1.3 1.0 %copy.15.pattern = s32[1536,2]{1,0:T(8,128)S(1)} copy(s32[1536,2]{0,1:T(2,128)} %param.20) | data formatting | bytes 24576 | tf_op args[9]
  2.3 0.0 copy-start
  2.3 1.0 %copy-done = bf16[512,512]{1,0:T(8,128)(2,1)S(1)} copy-done((bf16[512,512]{1,0:T(8,128)(2,1)S(1)}, bf16[512,512]{1,0:T(8,128)(2,1)}, u32[]{:S(2)}) %copy-start) | copy-done | bytes 524312
  3.3 0.0 copy-start.1
  3.3 1.0 %copy-done.1 = bf16[512,512]{1,0:T(8,128)(2,1)S(1)} copy-done((bf16[512,512]{1,0:T(8,128)(2,1)S(1)}, bf16[512,512]{1,0:T(8,128)(2,1)}, u32[]{:S(2)}) %copy-start.1) | copy-done | bytes 524312
  4.4 0.0 copy-start.2
  4.4 1.0 %copy-done.2 = bf16[512,512]{1,0:T(8,128)(2,1)S(1)} copy-done((bf16[512,512]{1,0:T(8,128)(2,1)S(1)}, bf16[512,512]{1,0:T(8,128)(2,1)}, u32[]{:S(2)}) %copy-start.2) | copy-done | bytes 524312
  5.4 0.0 copy-start.3
  5.4 1.0 %copy-done.3 = bf16[512,512]{1,0:T(8,128)(2,1)S(1)} copy-done((bf16[512,512]{1,0:T(8,128)(2,1)S(1)}, bf16[512,512]{1,0:T(8,128)(2,1)}, u32[]{:S(2)}) %copy-start.3) | copy-done | bytes 524312
  6.5 0.0 copy-start.4
  6.5 0.9 %copy-done.4 = bf16[1,128,512]{2,1,0:T(8,128)(2,1)S(1)} copy-done((bf16[1,128,512]{2,1,0:T(8,128)(2,1)S(1)}, bf16[1,128,512]{2,1,0:T(8,128)(2,1)}, u32[]{:S(2)}) %copy-start.4) | copy-done | bytes 131096
  7.4 0.0 copy-start.5
  7.4 0.9 %copy-done.5 = bf16[1,128,512]{2,1,0:T(8,128)(2,1)S(1)} copy-done((bf16[1,128,512]{2,1,0:T(8,128)(2,1)S(1)}, bf16[1,128,512]{2,1,0:T(8,128)(2,1)}, u32[]{:S(2)}) %copy-start.5) | copy-done | bytes 131096
  8.3 0.0 copy-start.6
  8.3 0.7 %copy-done.6 = s32[1536,2]{0,1:T(2,128)S(1)} copy-done((s32[1536,2]{0,1:T(2,128)S(1)}, s32[1536,2]{0,1:T(2,128)}, u32[]{:S(2)}) %copy-start.6) | copy-done | bytes 12312
  9.0 0.0 copy-start.7
  9.0 0.7 copy-done.7
  9.6 0.0 copy-start.8
  9.6 0.7 copy-done.8
  10.3 50.4 %encoder_step.1 = (bf16[128,512]{1,0:T(8,128)(2,1)S(1)}, bf16[128,512]{1,0:T(8,128)(2,1)S(1)}, bf16[1536,512]{1,0:T(8,128)(2,1)}, f32[128,512]{1,0:T(8,128)S(1)}) custom-call(s32[12]{0:T(128)S(1)} %bitcast.13, s32[4]{0:T(128)S(1)} %copy-done.8, s32[1]{0:T(128)S(6)} %copy.20.live_s, s32[2,1536]{1,0:T(2,128)S(1)} %bitcast.12, s32[1536,2]{1,0:T(8,128)S(1)} %copy.15.pattern, ...), custom_call_target="tpu_custom_call" | custom-call | tf_op jit(solution)/shard_map/encoder_step/pallas_call | solution.py:514
  60.7 0.7 %copy.21 = bf16[1,128,512]{2,1,0:T(8,128)(2,1)} copy(bf16[1,128,512]{2,1,0:T(8,128)(2,1)S(1)} %bitcast.11) | data formatting | bytes 262144
  61.4 0.7 %copy.22 = bf16[1,128,512]{2,1,0:T(8,128)(2,1)} copy(bf16[1,128,512]{2,1,0:T(8,128)(2,1)S(1)} %bitcast.10) | data formatting | bytes 262144
  62.0 2.7 %copy.23 = bf16[1,1536,512]{2,1,0:T(8,128)(2,1)} copy(bf16[1,1536,512]{2,1,0:T(8,128)(2,1)} %bitcast.14) | data formatting | bytes 3145728
  64.7 0.7 %copy.24 = f32[128,512]{1,0:T(8,128)} copy(f32[128,512]{1,0:T(8,128)S(1)} %get-tuple-element.19) | data formatting | bytes 524288
Async XLA Ops:
  2.3 1.0 %copy-start = (bf16[512,512]{1,0:T(8,128)(2,1)S(1)}, bf16[512,512]{1,0:T(8,128)(2,1)}, u32[]{:S(2)}) copy-start(bf16[512,512]{1,0:T(8,128)(2,1)} %wm_h.1) | copy-start | bytes 1572868
  3.3 1.0 %copy-start.1 = (bf16[512,512]{1,0:T(8,128)(2,1)S(1)}, bf16[512,512]{1,0:T(8,128)(2,1)}, u32[]{:S(2)}) copy-start(bf16[512,512]{1,0:T(8,128)(2,1)} %ws_h.1) | copy-start | bytes 1572868
  4.4 1.0 %copy-start.2 = (bf16[512,512]{1,0:T(8,128)(2,1)S(1)}, bf16[512,512]{1,0:T(8,128)(2,1)}, u32[]{:S(2)}) copy-start(bf16[512,512]{1,0:T(8,128)(2,1)} %wa_h.1) | copy-start | bytes 1572868
  5.4 1.0 %copy-start.3 = (bf16[512,512]{1,0:T(8,128)(2,1)S(1)}, bf16[512,512]{1,0:T(8,128)(2,1)}, u32[]{:S(2)}) copy-start(bf16[512,512]{1,0:T(8,128)(2,1)} %wo_h.1) | copy-start | bytes 1572868
  6.5 0.9 %copy-start.4 = (bf16[1,128,512]{2,1,0:T(8,128)(2,1)S(1)}, bf16[1,128,512]{2,1,0:T(8,128)(2,1)}, u32[]{:S(2)}) copy-start(bf16[1,128,512]{2,1,0:T(8,128)(2,1)} %param.12) | copy-start | bytes 393220
  7.4 0.9 %copy-start.5 = (bf16[1,128,512]{2,1,0:T(8,128)(2,1)S(1)}, bf16[1,128,512]{2,1,0:T(8,128)(2,1)}, u32[]{:S(2)}) copy-start(bf16[1,128,512]{2,1,0:T(8,128)(2,1)} %param.13) | copy-start | bytes 393220
  8.3 0.7 %copy-start.6 = (s32[1536,2]{0,1:T(2,128)S(1)}, s32[1536,2]{0,1:T(2,128)}, u32[]{:S(2)}) copy-start(s32[1536,2]{0,1:T(2,128)} %param.20) | copy-start | bytes 36868
  9.0 0.7 %copy-start.7 = (s32[12,1]{0,1:T(1,128)S(1)}, s32[12,1]{0,1:T(1,128)}, u32[]{:S(2)}) copy-start(s32[12,1]{0,1:T(1,128)} %param.18) | copy-start | bytes 148
  9.6 0.7 %copy-start.8 = (s32[4]{0:T(128)S(1)}, s32[4]{0:T(128)}, u32[]{:S(2)}) copy-start(s32[4]{0:T(128)} %owner_s.1) | copy-start | bytes 52

commit v2 on v1

--- a/solution.py
+++ b/solution.py
@@ -158,11 +158,10 @@
 def fused(
     bands,
     tile,
-    target_s,
-    owner_s,
-    live_s,
-    pattern_t,
-    pattern,
+    target_h,
+    owner_h,
+    live_h,
+    pattern_h,
     grid_h,
     mesh_h,
     cot_h,
@@ -174,6 +173,14 @@
     grad_mesh_h,
     grad_grid_h,
     wg_h,
+    mesh_out_v,
+    grad_mesh_v,
+    gg_v,
+    wg_v,
+    target_s,
+    owner_s,
+    live_s,
+    pattern_t,
     grid_v,
     mesh_v,
     cot_v,
@@ -191,9 +198,6 @@
     part_recv,
     dagg_all,
     dpm,
-    gg_v,
-    mesh_out_v,
-    grad_mesh_v,
     sums,
     send_a,
     recv_a,
@@ -202,7 +206,6 @@
     send_c,
     recv_c,
     total_c,
-    wg_v,
     in_sem,
     grid_sem,
     out_sem,
@@ -234,7 +237,18 @@
     loads = [
         pltpu.make_async_copy(src, dst, in_sem.at[i])
         for i, (src, dst) in enumerate(
-            ((wm_h, wm_v), (mesh_h, mesh_v), (cot_h, cot_v), (ws_h, ws_v), (wa_h, wa_v), (wo_h, wo_v))
+            (
+                (target_h, target_s),
+                (owner_h, owner_s),
+                (live_h, live_s),
+                (pattern_h, pattern_t),
+                (wm_h, wm_v),
+                (mesh_h, mesh_v),
+                (cot_h, cot_v),
+                (ws_h, ws_v),
+                (wa_h, wa_v),
+                (wo_h, wo_v),
+            )
         )
     ]
 
@@ -242,10 +256,11 @@
         rows = pl.ds(t * tile, tile)
         return pltpu.make_async_copy(grid_h.at[rows], grid_v.at[rows], grid_sem.at[t])
 
-    loads[0].start()
+    for load in loads[:5]:
+        load.start()
     for t in range(tiles):
         grid_load(t).start()
-    for load in loads[1:]:
+    for load in loads[5:]:
         load.start()
 
     barrier = pltpu.get_barrier_semaphore()
@@ -256,6 +271,8 @@
     pl.semaphore_signal(barrier, inc=1, device_id={"dp": core_mate}, device_id_type=MESH)
     pl.semaphore_signal(barrier, inc=1, device_id={"dp": x_mate}, device_id_type=MESH)
 
+    for load in loads[:4]:
+        load.wait()
     live = live_s[0]
     offsets = []
     for k in range(blocks):
@@ -270,16 +287,9 @@
             (row_ids == first).astype(F32) + (row_ids == second).astype(F32)
         ).astype(BF16)
 
-    loads[0].wait()
-
-    @pl.loop(0, tiles)
-    def _(t):
-        rows = pl.ds(pl.multiple_of(t * tile, tile), tile)
+    loads[4].wait()
+    for t in range(tiles):
         grid_load(t).wait()
-        pre = mm(grid_v[rows, :], wm_v[...])
-        gate = logistic_of(pre)
-        msgs[rows, :] = (pre * gate).astype(BF16)
-        slope[rows, :] = gate * (1.0 + pre * (1.0 - gate))
 
     def part_copy(h, rel):
         other = (me + rel) % bands
@@ -295,7 +305,16 @@
     rels = (2, 1, 3)
     for h in range(2):
         cols = slice(h * half, (h + 1) * half)
-        partial = mm(hits[...], msgs[:, cols])
+
+        @pl.loop(0, tiles)
+        def _(t):
+            rows = pl.ds(pl.multiple_of(t * tile, tile), tile)
+            pre = mm(grid_v[rows, :], wm_v[:, cols])
+            gate = logistic_of(pre)
+            msgs[h, rows, :] = (pre * gate).astype(BF16)
+            slope[h, rows, :] = gate * (1.0 + pre * (1.0 - gate))
+
+        partial = mm(hits[...], msgs[h])
         part[:, cols] = partial
         part_send[h] = partial.astype(BF16)
         if h == 0:
@@ -303,21 +322,15 @@
         for rel in rels:
             part_copy(h, rel).start()
 
-    for load in loads[1:]:
+    for load in loads[5:]:
         load.wait()
     mesh_rows_v = mesh_v[...]
     cot_rows = cot_v[...]
     pre_self = mm(mesh_rows_v, ws_v[...])
     d_hidden = mm_t(cot_rows, wo_v[...])
 
-    col_ids = lax.broadcasted_iota(jnp.int32, (block, mesh_rows), 1)
-    for k in range(blocks):
-        rows = pl.ds(k * block, block)
-        first = pattern[rows, 0:1] + offsets[k]
-        second = pattern[rows, 1:2] + offsets[k]
-        hits_t[rows, :] = (
-            (col_ids == first).astype(F32) + (col_ids == second).astype(F32)
-        ).astype(BF16)
+    for t in range(tiles):
+        hits_t[t * tile : (t + 1) * tile, :] = hits[:, t * tile : (t + 1) * tile].T
     for t in range(tiles):
         grid_t[:, t * tile : (t + 1) * tile] = grid_v[t * tile : (t + 1) * tile, :].T
 
@@ -334,81 +347,89 @@
     gate = logistic_of(pre_hidden)
     hidden = (pre_hidden * gate).astype(BF16)
     dph = (d_hidden * (gate * (1.0 + pre_hidden * (1.0 - gate)))).astype(BF16)
-    dagg_all[own, :] = mm_t(dph, wa_v[...]).astype(BF16)
-
-    def dagg_copy(rel):
+
+    def dagg_copy(h, rel):
         return pltpu.make_async_remote_copy(
-            src_ref=dagg_all.at[own],
-            dst_ref=dagg_all.at[own],
-            send_sem=dagg_ss.at[rel - 1],
-            recv_sem=dagg_rs.at[rel - 1],
+            src_ref=dagg_all.at[h, own],
+            dst_ref=dagg_all.at[h, own],
+            send_sem=dagg_ss.at[h, rel - 1],
+            recv_sem=dagg_rs.at[h, rel - 1],
             device_id={"band": (me + rel) % bands},
             device_id_type=MESH,
         )
 
-    for rel in rels:
-        dagg_copy(rel).start()
-
-    def a_copy(b):
+    for h in range(2):
+        dagg_all[h, own, :] = mm_t(dph, wa_v[h * half : (h + 1) * half, :]).astype(BF16)
+        for rel in rels:
+            dagg_copy(h, rel).start()
+
+    def a_copy(b, h):
         return pltpu.make_async_remote_copy(
-            src_ref=send_a.at[b],
-            dst_ref=recv_a.at[b],
-            send_sem=a_ss.at[b],
-            recv_sem=a_rs.at[b],
+            src_ref=send_a.at[b, h],
+            dst_ref=recv_a.at[b, h],
+            send_sem=a_ss.at[b, h],
+            recv_sem=a_rs.at[b, h],
             device_id={"dp": core_mate},
             device_id_type=MESH,
         )
 
-    def b_copy(b):
+    def b_copy(b, h):
         return pltpu.make_async_remote_copy(
-            src_ref=send_b.at[b],
-            dst_ref=recv_b.at[b],
-            send_sem=b_ss.at[b],
-            recv_sem=b_rs.at[b],
+            src_ref=send_b.at[b, h],
+            dst_ref=recv_b.at[b, h],
+            send_sem=b_ss.at[b, h],
+            recv_sem=b_rs.at[b, h],
             device_id={"dp": x_mate},
             device_id_type=MESH,
         )
 
-    def c_copy(rel):
+    def c_copy(rel, h):
         other = (me + rel) % bands
         return pltpu.make_async_remote_copy(
-            src_ref=send_c.at[other],
-            dst_ref=recv_c.at[rel - 1],
-            send_sem=c_ss.at[rel - 1],
-            recv_sem=c_rs.at[rel - 1],
+            src_ref=send_c.at[other, h],
+            dst_ref=recv_c.at[rel - 1, h],
+            send_sem=c_ss.at[rel - 1, h],
+            recv_sem=c_rs.at[rel - 1, h],
             device_id={"band": other},
             device_id_type=MESH,
         )
 
     share = width // 4
 
-    def share_of(b, x, c):
-        return sums[b, pl.ds(pl.multiple_of((x * 2 + c) * share, share), share), :]
-
-    def step_a(b):
+    def share_of(b, h, x, c):
+        return sums[b, h, pl.ds(pl.multiple_of((x * 2 + c) * share, share), share), :]
+
+    def step_a(b, h):
         for x in range(2):
-            send_a[b, x] = share_of(b, x, 1 - core).astype(BF16)
-        a_copy(b).start()
-
-    def step_b(b):
-        a_copy(b).wait_recv()
+            send_a[b, h, x] = share_of(b, h, x, 1 - core).astype(BF16)
+        a_copy(b, h).start()
+
+    def step_b(b, h):
+        a_copy(b, h).wait_recv()
         away = 1 - column
-        send_b[b] = (share_of(b, away, core) + recv_a[b, away].astype(F32)).astype(BF16)
-        b_copy(b).start()
-
-    def step_c(b):
-        kept = share_of(b, column, core) + recv_a[b, column].astype(F32)
-        b_copy(b).wait_recv()
-        kept = kept + recv_b[b].astype(F32)
-        total_c[b] = kept
-        send_c[b] = kept.astype(BF16)
-
-    sums[0] = row_product(mesh_rows_v, dph)
-    step_a(0)
-    sums[1] = row_product(agg, dph)
-    step_a(1)
-    sums[2] = row_product(hidden, cot_rows)
-    step_a(2)
+        send_b[b, h] = (share_of(b, h, away, core) + recv_a[b, h, away].astype(F32)).astype(BF16)
+        b_copy(b, h).start()
+
+    def step_c(b, h):
+        kept = share_of(b, h, column, core) + recv_a[b, h, column].astype(F32)
+        b_copy(b, h).wait_recv()
+        kept = kept + recv_b[b, h].astype(F32)
+        total_c[b, h] = kept
+        send_c[b, h] = kept.astype(BF16)
+
+    def send_last(h, is_last):
+        for rel in rels:
+            other = (me + rel) % bands
+
+            @pl.when((other == 3) if is_last else (other != 3))
+            def _():
+                c_copy(rel, h).start()
+
+    halves = [slice(h * half, (h + 1) * half) for h in range(2)]
+    for b, (left, right) in enumerate(((mesh_rows_v, dph), (agg, dph), (hidden, cot_rows))):
+        for h in range(2):
+            sums[b, h] = row_product(left, right[:, halves[h]])
+            step_a(b, h)
     mesh_out_v[...] = (mesh_rows_v.astype(F32) + mm(hidden, wo_v[...])).astype(BF16)
     grad_mesh_v[...] = (cot_rows.astype(F32) + mm_t(dph, ws_v[...])).astype(BF16)
     stores = [
@@ -418,27 +439,27 @@
     for store in stores:
         store.start()
     for b in range(3):
-        step_b(b)
-    for b in range(3):
-        step_c(b)
-    for rel in rels:
-        dagg_copy(rel).wait_recv()
-    for rel in rels:
-
-        @pl.when((me + rel) % bands != 3)
-        def _():
-            c_copy(rel).start()
-
-    @pl.loop(0, tiles)
-    def _(t):
-        rows = pl.ds(pl.multiple_of(t * tile, tile), tile)
-        d_msg = mm(hits_t[rows, :], dagg_all[...])
-        dpm[rows, :] = (d_msg * slope[rows, :]).astype(BF16)
+        for h in range(2):
+            step_b(b, h)
 
     for h in range(2):
-        cols = slice(h * half, (h + 1) * half)
-        sums[3, :, cols] = mm(grid_t[...], dpm[:, cols])
-    step_a(3)
+        for rel in rels:
+            dagg_copy(h, rel).wait_recv()
+
+        @pl.loop(0, tiles)
+        def _(t):
+            rows = pl.ds(pl.multiple_of(t * tile, tile), tile)
+            d_msg = mm(hits_t[rows, :], dagg_all[h])
+            dpm[rows, halves[h]] = (d_msg * slope[h, rows, :]).astype(BF16)
+
+        sums[3, h] = mm(grid_t[...], dpm[:, halves[h]])
+        step_a(3, h)
+        if h == 0:
+            step_b(3, 0)
+            for g in range(2):
+                for b in range(3):
+                    step_c(b, g)
+                send_last(g, False)
 
     def gg_store(t):
         rows = pl.ds(pl.multiple_of(t * tile, tile), tile)
@@ -451,25 +472,22 @@
             gg_v[rows, :] = mm_t(dpm[rows, :], wm_v[...]).astype(BF16)
             gg_store(t).start()
 
-    grid_grads(0, tiles // 3)
-    step_b(3)
-    grid_grads(tiles // 3, tiles)
-    step_c(3)
-    for rel in rels:
-
-        @pl.when((me + rel) % bands == 3)
-        def _():
-            c_copy(rel).start()
-
-    total = total_c[me]
-    for rel in rels:
-        c_copy(rel).wait_recv()
-        total = total + recv_c[rel - 1].astype(F32)
-    wg_v[...] = total
-    last = pltpu.make_async_copy(wg_v, wg_h, out_sem.at[2])
-    last.start()
-    for store in stores:
-        store.wait()
+    step_c(3, 0)
+    send_last(0, True)
+    step_b(3, 1)
+    grid_grads(0, tiles // 2)
+    step_c(3, 1)
+    send_last(1, True)
+    grid_grads(tiles // 2, tiles)
+
+    for h in range(2):
+        total = total_c[me, h]
+        for rel in rels:
+            c_copy(rel, h).wait_recv()
+            total = total + recv_c[rel - 1, h].astype(F32)
+        wg_v[:, halves[h]] = total
+    stores.append(pltpu.make_async_copy(wg_v, wg_h, out_sem.at[2]))
+    stores[2].start()
 
     @pl.loop(0, tiles)
     def _(t):
@@ -478,12 +496,24 @@
     for rel in rels:
         for h in range(2):
             part_copy(h, rel).wait_send()
-        dagg_copy(rel).wait_send()
-        c_copy(rel).wait_send()
+            dagg_copy(h, rel).wait_send()
+            c_copy(rel, h).wait_send()
     for b in range(4):
-        a_copy(b).wait_send()
-        b_copy(b).wait_send()
-    last.wait()
+        for h in range(2):
+            a_copy(b, h).wait_send()
+            b_copy(b, h).wait_send()
+    for store in stores:
+        store.wait()
+
+
+def store_all(*refs):
+    count = len(refs) // 2
+    sems = refs[-1]
+    copies = [pltpu.make_async_copy(refs[i], refs[count + i], sems.at[i]) for i in range(count)]
+    for copy in copies:
+        copy.start()
+    for copy in copies:
+        copy.wait()
 
 
 def fused_shards(
@@ -508,66 +538,71 @@
     half = width // 2
     share = width // 4
     anywhere = pl.BlockSpec(memory_space=pl.ANY)
-    scalars = pl.BlockSpec(memory_space=pltpu.SMEM)
-    local = pl.BlockSpec(memory_space=pltpu.VMEM)
+    hbm = pl.BlockSpec(memory_space=pltpu.HBM)
     dma = pltpu.SemaphoreType.DMA
-    mesh_out, grad_mesh, grad_grid, weight_grads = pl.pallas_call(
+    vmem = pltpu.VMEM
+    shapes = (
+        jax.ShapeDtypeStruct((block, width), BF16),
+        jax.ShapeDtypeStruct((block, width), BF16),
+        jax.ShapeDtypeStruct((nodes, width), BF16),
+        jax.ShapeDtypeStruct((share, width), F32),
+    )
+    results = pl.pallas_call(
         functools.partial(fused, bands, tile),
-        out_shape=(
-            jax.ShapeDtypeStruct((block, width), BF16),
-            jax.ShapeDtypeStruct((block, width), BF16),
-            jax.ShapeDtypeStruct((nodes, width), BF16),
-            jax.ShapeDtypeStruct((share, width), F32),
-        ),
-        in_specs=[scalars] * 3 + [local] * 2 + [anywhere] * 7,
+        out_shape=shapes,
+        in_specs=[hbm] * 11,
         out_specs=(anywhere,) * 4,
         scratch_shapes=[
-            pltpu.VMEM((nodes, width), BF16),
-            pltpu.VMEM((block, width), BF16),
-            pltpu.VMEM((block, width), BF16),
-            pltpu.VMEM((width, width), BF16),
-            pltpu.VMEM((width, width), BF16),
-            pltpu.VMEM((width, width), BF16),
-            pltpu.VMEM((width, width), BF16),
-            pltpu.VMEM((rows, nodes), BF16),
-            pltpu.VMEM((nodes, rows), BF16),
-            pltpu.VMEM((width, nodes), BF16),
-            pltpu.VMEM((nodes, width), BF16),
-            pltpu.VMEM((nodes, width), F32),
-            pltpu.VMEM((rows, width), F32),
-            pltpu.VMEM((2, rows, half), BF16),
-            pltpu.VMEM((2, bands - 1, block, half), BF16),
-            pltpu.VMEM((rows, width), BF16),
-            pltpu.VMEM((nodes, width), BF16),
-            pltpu.VMEM((nodes, width), BF16),
-            pltpu.VMEM((block, width), BF16),
-            pltpu.VMEM((block, width), BF16),
-            pltpu.VMEM((4, width, width), F32),
-            pltpu.VMEM((4, 2, share, width), BF16),
-            pltpu.VMEM((4, 2, share, width), BF16),
-            pltpu.VMEM((4, share, width), BF16),
-            pltpu.VMEM((4, share, width), BF16),
-            pltpu.VMEM((4, share, width), BF16),
-            pltpu.VMEM((bands - 1, share, width), BF16),
-            pltpu.VMEM((4, share, width), F32),
-            pltpu.VMEM((share, width), F32),
-            dma((6,)),
+            vmem((block, width), BF16),
+            vmem((block, width), BF16),
+            vmem((nodes, width), BF16),
+            vmem((share, width), F32),
+            pltpu.SMEM(target.shape[:1], jnp.int32),
+            pltpu.SMEM(owner_map.shape, jnp.int32),
+            pltpu.SMEM(live_blocks.shape, jnp.int32),
+            vmem((2, nodes), jnp.int32),
+            vmem((nodes, width), BF16),
+            vmem((block, width), BF16),
+            vmem((block, width), BF16),
+            vmem((width, width), BF16),
+            vmem((width, width), BF16),
+            vmem((width, width), BF16),
+            vmem((width, width), BF16),
+            vmem((rows, nodes), BF16),
+            vmem((nodes, rows), BF16),
+            vmem((width, nodes), BF16),
+            vmem((2, nodes, half), BF16),
+            vmem((2, nodes, half), F32),
+            vmem((rows, width), F32),
+            vmem((2, rows, half), BF16),
+            vmem((2, bands - 1, block, half), BF16),
+            vmem((2, rows, half), BF16),
+            vmem((nodes, width), BF16),
+            vmem((4, 2, width, half), F32),
+            vmem((4, 2, 2, share, half), BF16),
+            vmem((4, 2, 2, share, half), BF16),
+            vmem((4, 2, share, half), BF16),
+            vmem((4, 2, share, half), BF16),
+            vmem((4, 2, share, half), BF16),
+            vmem((bands - 1, 2, share, half), BF16),
+            vmem((4, 2, share, half), F32),
+            dma((10,)),
             dma((tiles,)),
             dma((3,)),
             dma((tiles,)),
             dma((2, bands - 1)),
             dma((2, bands - 1)),
-            dma((bands - 1,)),
-            dma((bands - 1,)),
-            dma((4,)),
-            dma((4,)),
-            dma((4,)),
-            dma((4,)),
-            dma((bands - 1,)),
-            dma((bands - 1,)),
+            dma((2, bands - 1)),
+            dma((2, bands - 1)),
+            dma((4, 2)),
+            dma((4, 2)),
+            dma((4, 2)),
+            dma((4, 2)),
+            dma((bands - 1, 2)),
+            dma((bands - 1, 2)),
         ],
         compiler_params=pltpu.CompilerParams(
-            collective_id=0, has_side_effects=True, vmem_limit_bytes=50 * 2**20
+            collective_id=0, has_side_effects=True, vmem_limit_bytes=64 * 2**20
         ),
         name="encoder_step",
     )(
@@ -575,7 +610,6 @@
         owner_map,
         live_blocks,
         pattern.T,
-        pattern,
         grid_latent[0],
         mesh_latent[0],
         cotangent[0],
@@ -584,6 +618,15 @@
         w_agg,
         w_out,
     )
+    mesh_out, grad_mesh, grad_grid, weight_grads = pl.pallas_call(
+        store_all,
+        out_shape=shapes,
+        in_specs=[anywhere] * 4,
+        out_specs=(hbm,) * 4,
+        scratch_shapes=[dma((4,))],
+        compiler_params=pltpu.CompilerParams(vmem_limit_bytes=64 * 2**20),
+        name="store_results",
+    )(*results)
     return mesh_out[None], grad_mesh[None], grad_grid[None], weight_grads
 
 

time: 65.9 us -> 111 us (1.68)
  Pallas kernels: 50.4 us -> 110 us
  local copies, waits for them, and re-layouts: 13.6 us -> 0 us
    pallas_call x1 -> x2, Pallas kernels: 50.4 us -> 110 us  [the longest x1 64.7 us: fused_shards(): pl.pallas_call(store_all, out_shape=shapes, in_specs=[anywhere] * 4, out_...]
    unnamed x23 -> x0, local copies, waits for them, and re-layouts: 13.6 us -> none
where the time goes in v2:
time: 111 us
  Pallas kernels  110 us (99%)
  between operations  1.29 us (1%)
    pallas_call x1, Pallas kernels, fused_shards(): pl.pallas_call(store_all, out_shape=shapes, in_specs=[anywhere] * 4, out_...  64.7 us
    pallas_call x1, Pallas kernels, fused_shards(): pl.pallas_call(functools.partial(fused, bands, tile), out_shape=shapes, i...  45.2 us

profile of v2, /device:TPU:28, one launch (start us, length us, event | category | flops | bytes accessed | tf_op | source)
XLA Modules:
  0.0 111.2 jit_solution(6043847832757041086)
XLA Ops:
  1.3 45.2 %encoder_step.1 = (bf16[128,512]{1,0:T(8,128)(2,1)}, bf16[128,512]{1,0:T(8,128)(2,1)}, bf16[1536,512]{1,0:T(8,128)(2,1)}, f32[128,512]{1,0:T(8,128)}) custom-call(s32[12]{0:T(128)} %bitcast.12, s32[4]{0:T(128)} %owner_h.1, s32[1]{0:T(128)S(6)} %copy.15.live_h, s32[2,1536]{1,0:T(2,128)} %bitcast.11, bf16[1536,512]{1,0:T(8,128)(2,1)} %bitcast.8, ...), custom_call_target="tpu_custom_call" | custom-call | tf_op jit(solution)/shard_map/encoder_step/pallas_call | solution.py:550
  46.5 64.7 %store_results.1 = (bf16[128,512]{1,0:T(8,128)(2,1)}, bf16[128,512]{1,0:T(8,128)(2,1)}, bf16[1536,512]{1,0:T(8,128)(2,1)}, f32[128,512]{1,0:T(8,128)}) custom-call(bf16[128,512]{1,0:T(8,128)(2,1)} %get-tuple-element.12.refs_0_, bf16[128,512]{1,0:T(8,128)(2,1)} %get-tuple-element.13.refs_1_, bf16[1536,512]{1,0:T(8,128)(2,1)} %get-tuple-element.14.refs_2_, ...), custom_call_target="tpu_custom_call" | custom-call | tf_op jit(solution)/shard_map/store_results/pallas_call | solution.py:621

commit v3 on v2

--- a/solution.py
+++ b/solution.py
@@ -506,14 +506,26 @@
         store.wait()
 
 
-def store_all(*refs):
-    count = len(refs) // 2
-    sems = refs[-1]
-    copies = [pltpu.make_async_copy(refs[i], refs[count + i], sems.at[i]) for i in range(count)]
-    for copy in copies:
-        copy.start()
-    for copy in copies:
-        copy.wait()
+def store_all(chunk, *refs):
+    sources, targets, stages, sems = refs[:4], refs[4:8], refs[8:12], refs[12]
+    pairs = []
+    for source, target, stage in zip(sources, targets, stages):
+        for low in range(0, source.shape[0], chunk):
+            rows = pl.ds(low, min(chunk, source.shape[0]))
+            sem = sems.at[len(pairs)]
+            pairs.append(
+                (
+                    pltpu.make_async_copy(source.at[rows], stage.at[rows], sem),
+                    pltpu.make_async_copy(stage.at[rows], target.at[rows], sem),
+                )
+            )
+    for load, _ in pairs:
+        load.start()
+    for load, store in pairs:
+        load.wait()
+        store.start()
+    for _, store in pairs:
+        store.wait()
 
 
 def fused_shards(
@@ -618,12 +630,14 @@
         w_agg,
         w_out,
     )
+    chunk = 2 * tile
     mesh_out, grad_mesh, grad_grid, weight_grads = pl.pallas_call(
-        store_all,
+        functools.partial(store_all, chunk),
         out_shape=shapes,
         in_specs=[anywhere] * 4,
         out_specs=(hbm,) * 4,
-        scratch_shapes=[dma((4,))],
+        scratch_shapes=[vmem(shape.shape, shape.dtype) for shape in shapes]
+        + [dma((3 + nodes // chunk,))],
         compiler_params=pltpu.CompilerParams(vmem_limit_bytes=64 * 2**20),
         name="store_results",
     )(*results)

time: 111 us -> 49.3 us (0.44)
  Pallas kernels: 110 us -> 47.6 us
    pallas_call x1, Pallas kernels: 64.7 us -> 2.45 us  [fused_shards(): pl.pallas_call(functools.partial(store_all, chunk), out_shape=shapes, in_...]
where the time goes in v3:
time: 49.3 us; the launch traced here: 48.9 us
  Pallas kernels  47.6 us (97%)
  between operations  1.29 us (3%)
    pallas_call x1, Pallas kernels, fused_shards(): pl.pallas_call(functools.partial(fused, bands, tile), out_shape=shapes, i...  45.2 us
    pallas_call x1, Pallas kernels, fused_shards(): pl.pallas_call(functools.partial(store_all, chunk), out_shape=shapes, in_...  2.45 us

profile of v3, /device:TPU:28, one launch (start us, length us, event | category | flops | bytes accessed | tf_op | source)
XLA Modules:
  0.0 48.9 jit_solution(14856598917976759198)
XLA Ops:
  1.3 45.2 %encoder_step.1 = (bf16[128,512]{1,0:T(8,128)(2,1)}, bf16[128,512]{1,0:T(8,128)(2,1)}, bf16[1536,512]{1,0:T(8,128)(2,1)}, f32[128,512]{1,0:T(8,128)}) custom-call(s32[12]{0:T(128)} %bitcast.12, s32[4]{0:T(128)} %owner_h.1, s32[1]{0:T(128)S(6)} %copy.15.live_h, s32[2,1536]{1,0:T(2,128)} %bitcast.11, bf16[1536,512]{1,0:T(8,128)(2,1)} %bitcast.8, ...), custom_call_target="tpu_custom_call" | custom-call | tf_op jit(solution)/shard_map/encoder_step/pallas_call | solution.py:562
  46.5 2.5 %store_results.1 = (bf16[128,512]{1,0:T(8,128)(2,1)}, bf16[128,512]{1,0:T(8,128)(2,1)}, bf16[1536,512]{1,0:T(8,128)(2,1)}, f32[128,512]{1,0:T(8,128)}) custom-call(bf16[128,512]{1,0:T(8,128)(2,1)} %get-tuple-element.12.refs_0_, bf16[128,512]{1,0:T(8,128)(2,1)} %get-tuple-element.13.refs_1_, bf16[1536,512]{1,0:T(8,128)(2,1)} %get-tuple-element.14.refs_2_, ...), custom_call_target="tpu_custom_call" | custom-call | tf_op jit(solution)/shard_map/store_results/pallas_call | solution.py:634

commit v4 on v3

--- a/solution.py
+++ b/solution.py
@@ -446,9 +446,9 @@
         for rel in rels:
             dagg_copy(h, rel).wait_recv()
 
-        @pl.loop(0, tiles)
+        @pl.loop(0, tiles // 2)
         def _(t):
-            rows = pl.ds(pl.multiple_of(t * tile, tile), tile)
+            rows = pl.ds(pl.multiple_of(t * (2 * tile), 2 * tile), 2 * tile)
             d_msg = mm(hits_t[rows, :], dagg_all[h])
             dpm[rows, halves[h]] = (d_msg * slope[h, rows, :]).astype(BF16)
 

time: 49.3 us -> 49 us (level)
  no operation moved by 1% of the time
where the time goes in v4:
time: 49 us; the launch traced here: 48.6 us
  Pallas kernels  47.3 us (97%)
  between operations  1.29 us (3%)
    pallas_call x1, Pallas kernels, fused_shards(): pl.pallas_call(functools.partial(fused, bands, tile), out_shape=shapes, i...  44.9 us
    pallas_call x1, Pallas kernels, fused_shards(): pl.pallas_call(functools.partial(store_all, chunk), out_shape=shapes, in_...  2.45 us

profile of v4, /device:TPU:28, one launch (start us, length us, event | category | flops | bytes accessed | tf_op | source)
XLA Modules:
  0.0 48.6 jit_solution(1359318149882441932)
XLA Ops:
  1.3 44.9 %encoder_step.1 = (bf16[128,512]{1,0:T(8,128)(2,1)}, bf16[128,512]{1,0:T(8,128)(2,1)}, bf16[1536,512]{1,0:T(8,128)(2,1)}, f32[128,512]{1,0:T(8,128)}) custom-call(s32[12]{0:T(128)} %bitcast.12, s32[4]{0:T(128)} %owner_h.1, s32[1]{0:T(128)S(6)} %copy.15.live_h, s32[2,1536]{1,0:T(2,128)} %bitcast.11, bf16[1536,512]{1,0:T(8,128)(2,1)} %bitcast.8, ...), custom_call_target="tpu_custom_call" | custom-call | tf_op jit(solution)/shard_map/encoder_step/pallas_call | solution.py:562
  46.2 2.5 %store_results.1 = (bf16[128,512]{1,0:T(8,128)(2,1)}, bf16[128,512]{1,0:T(8,128)(2,1)}, bf16[1536,512]{1,0:T(8,128)(2,1)}, f32[128,512]{1,0:T(8,128)}) custom-call(bf16[128,512]{1,0:T(8,128)(2,1)} %get-tuple-element.12.refs_0_, bf16[128,512]{1,0:T(8,128)(2,1)} %get-tuple-element.13.refs_1_, bf16[1536,512]{1,0:T(8,128)(2,1)} %get-tuple-element.14.refs_2_, ...), custom_call_target="tpu_custom_call" | custom-call | tf_op jit(solution)/shard_map/store_results/pallas_call | solution.py:634
